TPU v7x, 128 devices: a whole 4x4x4 slice. The times are simulated.
128 devices in a mesh: feat: 8 (over x, core), rows: 16 (over z, y).
Axes of the slice: x: 4, y: 4, z: 4, core: 2. Of those that a mesh axis runs over, the one named last changes fastest.
Arguments:
- features: bfloat16 [128, 128, 768], P('feat', None, 'rows'), may hold values from -6 to 6
- w_in: bfloat16 [128, 256], replicated, may hold values from -0.5 to 0.5
- bias: float32 [256], replicated, may hold values from -4 to 4
- tiles: bfloat16 [768, 8, 128, 128], P(('feat', 'rows')), may hold values from 0 to 1, as said below
- tile_cols: int32 [768, 8], P(('feat', 'rows')), may hold values from 0 to 767, as said below
- tile_counts: int32 [768], P(('feat', 'rows')), may hold values from 1 to 8, as said below
- cotangent: bfloat16 [98304, 256], P(('feat', 'rows')), may hold values from -6 to 6
Outputs:
- hidden: bfloat16 [98304, 256], P(('feat', 'rows'))
- weight_grad: float32 [128, 256], P('feat')
Inputs may be any that keep to these rules, and one draw needn't show every extreme that they name: Each block row's count lies between 1 and 8; in every draw some device owns a block row with 8 live slots. Slots k >= tile_counts[I] are ignored. `tile_cols`: block row I on the device owning blocks s * 6 to s * 6 + 6 - 1 (s = I // 6) names column blocks J with J // 96 = I // 96 and (J - (s % 16) * 6 + 2) mod 96 below 10: its own blocks or up to 2 blocks of the neighbouring devices in its cycle, wrapping; both ends are reached. `tiles`: entries are 0 or 1.
All inputs are finite; a program needn't handle non-finite values.
Results may differ from a plain program's by a relative error of at most 0.008.
Values may be sent and summed in bfloat16 or wider, within the bound.
No kernel may reach another device: no remote copies, remote signals or barrier semaphores. Data moves between devices by JAX's collectives and lax.ppermute only.
A program may use at most 64 MiB of HBM per device.

v0:
```python
import jax
import jax.numpy as jnp
from jax import lax
from jax.sharding import PartitionSpec as P

HALO_BLK = 2


def padded(cells, sides, width):
    for axis, dim in sides:
        count = lax.axis_size(axis)
        head = lax.slice_in_dim(cells, 0, width, axis=dim)
        tail = lax.slice_in_dim(cells, cells.shape[dim] - width, cells.shape[dim], axis=dim)
        cells = jnp.concatenate(
            [
                lax.ppermute(tail, axis, [(i, (i + 1) % count) for i in range(count)]),
                cells,
                lax.ppermute(head, axis, [((i + 1) % count, i) for i in range(count)]),
            ],
            axis=dim,
        )
    return cells


def shifted(block, axis, distance):
    devices = range(lax.axis_size(axis))
    route = [((i - distance) % len(devices), i) for i in devices]
    return lax.ppermute(block, axis, route)


def gelu_parts(values):
    inner = 0.7978845608 * (values + 0.044715 * values * values * values)
    tangent = jnp.tanh(inner)
    output = 0.5 * values * (1.0 + tangent)
    slope = 0.5 * (1.0 + tangent) + 0.5 * values * (1.0 - tangent * tangent) * 0.7978845608 * (
        1.0 + 3.0 * 0.044715 * values * values
    )
    return (output, slope)


def halo_projected(projected, margin):
    return padded(projected, (("rows", 0),), margin)


def body(features, w_in, bias, tiles, tile_cols, tile_counts, cotangent):
    block_rows, slot_count, tile_side, unused_side = tiles.shape
    hidden_width = w_in.shape[1]
    feat_size = lax.axis_size("feat")
    row_size = lax.axis_size("rows")
    slice_width = w_in.shape[0] // feat_size
    nodes_dev = block_rows * tile_side
    sub_rows = nodes_dev // row_size
    feat_id = lax.axis_index("feat")
    row_id = lax.axis_index("rows")
    margin = HALO_BLK * tile_side
    w_own = lax.dynamic_slice_in_dim(w_in, feat_id * slice_width, slice_width, 0)
    partial_value = jnp.einsum(
        "cdn,ch->dnh", features, w_own, preferred_element_type=jnp.float32
    ).astype(jnp.bfloat16)
    received = lax.all_to_all(
        partial_value, ("feat", "rows"), split_axis=0, concat_axis=0, tiled=True
    )
    received = received.reshape(feat_size, nodes_dev, hidden_width)
    projected = jnp.sum(received.astype(jnp.float32), axis=0).astype(jnp.bfloat16)
    extended = halo_projected(projected, margin)
    ext_count = block_rows + 2 * HALO_BLK
    ext_blocks = extended.reshape(ext_count, tile_side, hidden_width)
    cycle_size = block_rows * row_size
    local_cols = (tile_cols - feat_id * cycle_size - row_id * block_rows + HALO_BLK) % cycle_size
    slot_ids = jnp.arange(slot_count, dtype=jnp.int32)
    live_slot = (slot_ids[None, :] < tile_counts[:, None]).astype(jnp.bfloat16)
    masked = tiles * live_slot[:, :, None, None]
    degree = jnp.sum(masked, axis=(1, 3), dtype=jnp.float32)
    neighbours = ext_blocks[local_cols]
    summed_rows = jnp.einsum(
        "bkij,bkjh->bih", masked, neighbours, preferred_element_type=jnp.float32
    )
    own_rows = projected.reshape(block_rows, tile_side, hidden_width).astype(jnp.float32)
    pre_act = (own_rows + summed_rows) / (degree[:, :, None] + 1.0) + bias
    activated, slope = gelu_parts(pre_act)
    hidden = activated.astype(jnp.bfloat16).reshape(nodes_dev, hidden_width)
    scaled = (
        cotangent.reshape(block_rows, tile_side, hidden_width).astype(jnp.float32)
        * slope
        / (degree[:, :, None] + 1.0)
    ).astype(jnp.bfloat16)
    targets = jnp.arange(ext_count, dtype=jnp.int32)
    onehot = (local_cols[:, :, None] == targets[None, None, :]).astype(jnp.bfloat16)
    combined = jnp.einsum(
        "bkq,bkij->qbij", onehot, masked, preferred_element_type=jnp.float32
    ).astype(jnp.bfloat16)
    ext_sums = jnp.einsum("qbij,bih->qjh", combined, scaled, preferred_element_type=jnp.float32)
    from_before = shifted(ext_sums[block_rows + HALO_BLK :].astype(jnp.bfloat16), "rows", 1).astype(
        jnp.float32
    )
    from_after = shifted(ext_sums[:HALO_BLK].astype(jnp.bfloat16), "rows", -1).astype(jnp.float32)
    own_sums = ext_sums[HALO_BLK : HALO_BLK + block_rows] + scaled.astype(jnp.float32)
    own_sums = own_sums.at[:HALO_BLK].add(from_before)
    own_sums = own_sums.at[block_rows - HALO_BLK :].add(from_after)
    grad_proj = own_sums.astype(jnp.bfloat16).reshape(nodes_dev, hidden_width)
    pieces = lax.all_to_all(
        grad_proj.reshape(row_size, sub_rows, hidden_width),
        "rows",
        split_axis=0,
        concat_axis=0,
        tiled=True,
    )
    grad_slice = jnp.einsum(
        "cdn,dnh->ch",
        features,
        lax.all_gather(pieces, "feat", axis=0, tiled=True),
        preferred_element_type=jnp.float32,
    )
    weight_grad = lax.psum(grad_slice, "rows")
    return (hidden, weight_grad)


def solution(mesh):
    in_specs = (
        P("feat", None, "rows"),
        P(),
        P(),
        P(("feat", "rows"), None, None, None),
        P(("feat", "rows"), None),
        P(("feat", "rows")),
        P(("feat", "rows"), None),
    )
    out_specs = (P(("feat", "rows"), None), P("feat", None))
    return jax.shard_map(body, mesh=mesh, in_specs=in_specs, out_specs=out_specs, check_vma=False)
```

profile of v0, /device:TPU:0, one launch (start us, length us, event | category | flops | bytes accessed | tf_op | source)
XLA Modules:
  0.0 216.6 jit_solution(2524314712389904341)
XLA Ops:
  7.2 0.0 copy-start
  7.2 0.8 copy-done
  8.0 1.9 convert_bitcast_fusion.1
  9.9 3.2 %copy.17 = bf16[128,48,256]{2,1,0:T(8,128)(2,1)} copy(bf16[128,48,256]{0,2,1:T(8,128)(2,1)S(1)} %convert_bitcast_fusion.1) | data formatting | bytes 6291456 | tf_op jit(solution)/shard_map/convert_element_type | solution.py:59
  13.1 0.0 copy-start.9
  13.1 0.0 copy-start.8
  13.1 11.1 %all-to-all-start = ((bf16[128,48,256]{2,1,0:T(8,128)(2,1)}), bf16[128,48,256]{2,1,0:T(8,128)(2,1)S(1)}, u32[]{:S(2)}, u32[]{:S(2)}) async-start(bf16[128,48,256]{2,1,0:T(8,128)(2,1)} %copy.17), calls=%async_computation | async-start | bytes 6291456 | tf_op jit(solution)/shard_map/all_to_all | solution.py:60
  24.3 0.0 all-gather.2.cloned.1.call-start
  24.3 0.0 copy-done.9
  24.3 0.1 fusion.27
  24.4 0.0 copy-done.8
  24.4 2.0 convert_reduce_fusion
  26.5 0.0 copy-start.1
  26.5 1.1 copy-done.1
  27.6 3.1 %convert_bitcast_fusion = bf16[10,6,128,128]{3,0,2,1:T(8,128)(2,1)} fusion(bf16[6,8,128,128]{3,2,1,0:T(8,128)(2,1)S(1)} %get-tuple-element.27, s32[6,8]{1,0:T(8,128)S(1)} %get-tuple-element.29), kind=kOutput, calls=%fused_computation.2 | convolution fusion | flops 16712160 | bytes 3539136 | tf_op jit(solution)/shard_map/bkq,bkij->qbij/dot_general | solution.py:89
  30.7 33.8 %all-to-all-done = bf16[128,48,256]{2,1,0:T(8,128)(2,1)S(1)} async-done(((bf16[128,48,256]{2,1,0:T(8,128)(2,1)}), bf16[128,48,256]{2,1,0:T(8,128)(2,1)S(1)}, u32[]{:S(2)}, u32[]{:S(2)}) %all-to-all-start) | async-done | bytes 3145760 | tf_op jit(solution)/shard_map/all_to_all | solution.py:60
  64.5 0.4 bitcast_reduce_fusion
  64.9 0.0 copy-start.4
  65.0 0.7 copy-done.4
  65.7 0.7 collective-permute-start
  66.4 4.7 %collective-permute-start.1 = (bf16[256,256]{1,0:T(8,128)(2,1)S(1)}, bf16[256,256]{1,0:T(8,128)(2,1)S(1)}, u32[]{:S(2)}, u32[]{:S(2)}) collective-permute-start(bf16[256,256]{1,0:T(8,128)(2,1)S(1)} %get-tuple-element.35), channel_id=1, source_target_pairs={{1,0},{2,1},{3,2},{4,3},{5,4},{6,5},{7,6},{8,7},{9,8},{10,9},{11,1... | collective-permute-start | bytes 393224 | tf_op jit(solution)/shard_map/ppermute | solution.py:18
  71.1 0.1 reshape.114
  71.2 2.9 %collective-permute-done = bf16[256,256]{1,0:T(8,128)(2,1)S(1)} collective-permute-done((bf16[256,256]{1,0:T(8,128)(2,1)S(1)}, bf16[256,256]{1,0:T(8,128)(2,1)S(1)}, u32[]{:S(2)}, u32[]{:S(2)}) %collective-permute-start) | collective-permute-done | bytes 131104 | tf_op jit(solution)/shard_map/ppermute | solution.py:16
  74.1 0.0 collective-permute-done.1
  74.1 1.0 pad_maximum_fusion
  75.1 0.0 copy-start.2
  75.1 0.0 copy-start.5
  75.1 0.0 copy-start.10
  75.2 2.5 %gather_fusion = bf16[48,128,256]{2,1,0:T(8,128)(2,1)} fusion(bf16[10,128,256]{2,1,0:T(8,128)(2,1)S(1)} %bitcast.47, s32[1024]{0:T(1024)S(1)} %pad_clamp_fusion), kind=kCustom, calls=%fused_computation | custom fusion | bytes 6291648 | tf_op jit(solution)/shard_map/gather | solution.py:74
  77.7 0.0 copy-done.2
  77.7 0.0 copy-done.5
  77.7 0.0 copy-done.10
  77.7 0.0 copy-start.3
  77.7 0.0 copy-start.7
  77.7 2.8 %fusion.8 = f32[6,128,256]{2,1,0:T(8,128)S(1)} fusion(bf16[6,8,128,128]{3,2,1,0:T(8,128)(2,1)S(1)} %copy-done.2, bf16[6,8,128,256]{3,2,1,0:T(8,128)(2,1)} %bitcast.49, bf16[6,128,256]{2,1,0:T(8,128)(2,1)S(1)} %bitcast.50, f32[256]{0:T(256)S(1)} %copy-done.10, f32[6,128]{1,0:T(8,128)S(1)} %broadcast_add_fusion), kind=kOutput, calls=%fused_computation.12 | convolution fusion | flops 403439616 | bytes 5902336 | tf_op jit(solution)/shard_map/bkij,bkjh->bih/dot_general | solution.py:75
  80.5 0.0 copy-done.3
  80.5 0.1 copy-done.7
  80.6 1.5 fusion.32
  82.1 0.1 collective-permute-start.2
  82.2 0.0 copy-start.6
  82.2 1.4 slice_add_fusion
  83.6 5.3 %collective-permute-start.3 = (bf16[2,128,256]{2,1,0:T(8,128)(2,1)S(1)}, bf16[2,128,256]{2,1,0:T(8,128)(2,1)S(1)}, u32[]{:S(2)}, u32[]{:S(2)}) collective-permute-start(bf16[2,128,256]{2,1,0:T(8,128)(2,1)S(1)} %get-tuple-element.32), channel_id=1, source_target_pairs={{1,0},{2,1},{3,2},{4,3},{5,4},{6,5},{7,6},{8,7},{9,8},{10,9},{11,1... | collective-permute-start | bytes 393224 | tf_op jit(solution)/shard_map/ppermute | solution.py:28
  88.9 1.6 collective-permute-done.2
  90.5 0.1 fusion.19
  90.5 0.9 collective-permute-done.3
  91.4 0.1 fusion.18
  91.5 16.3 %all_to_all.10 = bf16[16,48,256]{2,1,0:T(8,128)(2,1)S(1)} all-to-all(bf16[16,48,256]{2,1,0:T(8,128)(2,1)S(1)} %bitcast.51), channel_id=1, replica_groups=mesh['feat'=8,'rows'=16] {'rows'}, dimensions={0} | all-to-all | bytes 786432 | tf_op jit(solution)/shard_map/all_to_all | solution.py:101
  107.9 0.9 copy.20
  108.8 0.0 all-gather.2.cloned.1.call-update
  108.8 24.0 %all-gather.2.cloned.1.call-done = bf16[128,48,256]{2,0,1:T(8,128)(2,1)} async-done(((bf16[16,48,256]{2,0,1:T(8,128)(2,1)}), bf16[128,48,256]{2,0,1:T(8,128)(2,1)}) %all-gather.2.cloned.1.call-update) | async-done | bytes 3145744 | tf_op jit(solution)/shard_map/all_gather | solution.py:111
  132.8 0.0 copy-done.6
  132.8 2.4 %convolution_bitcast_fusion.1 = f32[16,256]{1,0:T(8,128)S(1)} fusion(bf16[128,48,256]{2,0,1:T(8,128)(2,1)} %all-gather.2.cloned.1.call-done, bf16[16,128,48]{1,2,0:T(8,128)(2,1)S(1)} %copy-done.6), kind=kOutput, calls=%fused_computation.15 | convolution fusion | flops 50331648 | bytes 3358720 | tf_op jit(solution)/shard_map/cdn,dnh->ch/dot_general | solution.py:108
  135.2 74.5 %psum.7 = f32[16,256]{1,0:T(8,128)} all-reduce(f32[16,256]{1,0:T(8,128)S(1)} %convolution_bitcast_fusion.1), channel_id=1, replica_groups=mesh['feat'=8,'rows'=16] {'rows'}, use_global_device_ids=true, to_apply=%region_2.3 | all-reduce | flops 4096 | bytes 32768 | tf_op jit(solution)/shard_map/psum | solution.py:114
  (6 shorter events, 0.1 us)
Async XLA Ops:
  7.2 0.8 copy-start
  13.1 11.2 %copy-start.9 = (s32[6]{0:T(128)S(1)}, s32[6]{0:T(128)}, u32[]{:S(2)}) copy-start(s32[6]{0:T(128)} %param.16) | copy-start | bytes 76
  13.1 11.3 %copy-start.8 = (s32[6,8]{1,0:T(8,128)S(1)}, s32[6,8]{1,0:T(8,128)}, u32[]{:S(2)}) copy-start(s32[6,8]{1,0:T(8,128)} %param.15) | copy-start | bytes 580
  13.1 51.4 %all-to-all-start = ((bf16[128,48,256]{2,1,0:T(8,128)(2,1)}), bf16[128,48,256]{2,1,0:T(8,128)(2,1)S(1)}, u32[]{:S(2)}, u32[]{:S(2)}) async-start(bf16[128,48,256]{2,1,0:T(8,128)(2,1)} %copy.17), calls=%async_computation | async-start | bytes 6291456 | tf_op jit(solution)/shard_map/all_to_all | solution.py:60
  24.3 108.5 %all-gather.2.cloned.1.call-start = ((), (), s32[]{:S(2)}) async-start(), calls=%async_computation.2 | async-start | bytes 3538944 | tf_op jit(solution)/shard_map/all_gather | solution.py:111
  26.5 1.1 copy-start.1
  64.9 0.7 copy-start.4
  65.7 8.4 %collective-permute-start = (bf16[256,256]{1,0:T(8,128)(2,1)S(1)}, bf16[256,256]{1,0:T(8,128)(2,1)S(1)}, u32[]{:S(2)}, u32[]{:S(2)}) collective-permute-start(bf16[256,256]{1,0:T(8,128)(2,1)S(1)} %get-tuple-element.34), channel_id=1, source_target_pairs={{0,1},{1,2},{2,3},{3,4},{4,5},{5,6},{6,7},{7,8},{8,9},{9,10},{10,1... | collective-permute-start | bytes 393224 | tf_op jit(solution)/shard_map/ppermute | solution.py:16
  66.4 7.7 %collective-permute-start.1 = (bf16[256,256]{1,0:T(8,128)(2,1)S(1)}, bf16[256,256]{1,0:T(8,128)(2,1)S(1)}, u32[]{:S(2)}, u32[]{:S(2)}) collective-permute-start(bf16[256,256]{1,0:T(8,128)(2,1)S(1)} %get-tuple-element.35), channel_id=1, source_target_pairs={{1,0},{2,1},{3,2},{4,3},{5,4},{6,5},{7,6},{8,7},{9,8},{10,9},{11,1... | collective-permute-start | bytes 393224 | tf_op jit(solution)/shard_map/ppermute | solution.py:18
  75.1 2.6 %copy-start.2 = (bf16[6,8,128,128]{3,2,1,0:T(8,128)(2,1)S(1)}, bf16[6,8,128,128]{3,2,1,0:T(8,128)(2,1)}, u32[]{:S(2)}) copy-start(bf16[6,8,128,128]{3,2,1,0:T(8,128)(2,1)} %copy-done.1) | copy-start | bytes 4718596
  75.1 2.6 %copy-start.5 = (bf16[768,256]{1,0:T(8,128)(2,1)S(1)}, bf16[768,256]{1,0:T(8,128)(2,1)}, u32[]{:S(2)}) copy-start(bf16[768,256]{1,0:T(8,128)(2,1)} %copy-done.4) | copy-start | bytes 1179652
  75.1 2.6 %copy-start.10 = (f32[256]{0:T(256)S(1)}, f32[256]{0:T(256)}, u32[]{:S(2)}) copy-start(f32[256]{0:T(256)} %param.13) | copy-start | bytes 3076
  77.7 2.8 %copy-start.3 = (bf16[10,6,128,128]{3,0,2,1:T(8,128)(2,1)S(1)}, bf16[10,6,128,128]{3,0,2,1:T(8,128)(2,1)}, u32[]{:S(2)}) copy-start(bf16[10,6,128,128]{3,0,2,1:T(8,128)(2,1)} %convert_bitcast_fusion) | copy-start | bytes 5898244
  77.7 2.9 %copy-start.7 = (bf16[768,256]{1,0:T(8,128)(2,1)S(1)}, bf16[768,256]{1,0:T(8,128)(2,1)}, u32[]{:S(2)}) copy-start(bf16[768,256]{1,0:T(8,128)(2,1)} %param.17) | copy-start | bytes 1179652
  82.1 8.4 %collective-permute-start.2 = (bf16[2,128,256]{2,1,0:T(8,128)(2,1)S(1)}, bf16[2,128,256]{2,1,0:T(8,128)(2,1)S(1)}, u32[]{:S(2)}, u32[]{:S(2)}) collective-permute-start(bf16[2,128,256]{2,1,0:T(8,128)(2,1)S(1)} %get-tuple-element.33), channel_id=1, source_target_pairs={{15,0},{0,1},{1,2},{2,3},{3,4},{4,5},{5,6},{6,7},{7,8},{8,9},{9,10... | collective-permute-start | bytes 393224 | tf_op jit(solution)/shard_map/ppermute | solution.py:28
  82.2 50.6 %copy-start.6 = (bf16[16,128,48]{1,2,0:T(8,128)(2,1)S(1)}, bf16[16,128,48]{1,2,0:T(8,128)(2,1)}, u32[]{:S(2)}) copy-start(bf16[16,128,48]{1,2,0:T(8,128)(2,1)} %param.11) | copy-start | bytes 589828
  83.6 7.9 %collective-permute-start.3 = (bf16[2,128,256]{2,1,0:T(8,128)(2,1)S(1)}, bf16[2,128,256]{2,1,0:T(8,128)(2,1)S(1)}, u32[]{:S(2)}, u32[]{:S(2)}) collective-permute-start(bf16[2,128,256]{2,1,0:T(8,128)(2,1)S(1)} %get-tuple-element.32), channel_id=1, source_target_pairs={{1,0},{2,1},{3,2},{4,3},{5,4},{6,5},{7,6},{8,7},{9,8},{10,9},{11,1... | collective-permute-start | bytes 393224 | tf_op jit(solution)/shard_map/ppermute | solution.py:28
Sparse Core Ops, SparseCore 0:
  108.9 23.8 all-gather.1
where the time goes:
time: 217 us
  blocking collectives  90.9 us (42%)
  waiting for transfers between devices  63.2 us (29%)
  starting transfers between devices  22 us (10%)
  between operations  14.2 us (7%)
  matrix products  11.6 us (5%)
  local copies, waits for them, and re-layouts  9.55 us (4%)
  other arithmetic  5.11 us (2%)
    psum x1, blocking collectives, body(): weight_grad = lax.psum(grad_slice, 'rows')  74.5 us
    all_to_all x1, waiting for transfers between devices, body(): lax.all_to_all(partial_value, ('feat', 'rows'), split_axis=0, concat_axis...  33.8 us
    all_gather x1, waiting for transfers between devices, body(): lax.all_gather(pieces, 'feat', axis=0, tiled=True)  24 us
    all_to_all x1, blocking collectives, body(): lax.all_to_all(grad_proj.reshape(row_size, sub_rows, hidden_width), 'rows...  16.3 us
    all_to_all x1, starting transfers between devices, body(): lax.all_to_all(partial_value, ('feat', 'rows'), split_axis=0, concat_axis...  11.1 us
    ppermute x2, starting transfers between devices, shifted(): return lax.ppermute(block, axis, route)  5.42 us
    ppermute x1, starting transfers between devices, padded(): lax.ppermute(head, axis, [((i + 1) % count, i) for i in range(count)])  4.74 us
  transfers between devices with their start and end apart: 6, of which 5 were waited for; matrix products, arithmetic and copies ran while one was open for 3% of the time, Pallas kernels for 0%

commit v1 on v0

--- a/solution.py
+++ b/solution.py
@@ -2,6 +2,7 @@
 import jax.numpy as jnp
 from jax import lax
 from jax.sharding import PartitionSpec as P
+from jax.lax import all_gather
 
 HALO_BLK = 2
 
@@ -111,7 +112,7 @@
         lax.all_gather(pieces, "feat", axis=0, tiled=True),
         preferred_element_type=jnp.float32,
     )
-    weight_grad = lax.psum(grad_slice, "rows")
+    weight_grad = all_gather(grad_slice, axis_name="rows").sum(axis=0)
     return (hidden, weight_grad)
 
 

time: 217 us -> 167 us (0.77)
  blocking collectives: 90.9 us -> 40.3 us
    psum x1 -> x0, blocking collectives: 74.5 us -> none  [body(): weight_grad = lax.psum(grad_slice, 'rows')]
    all_gather x0 -> x1, blocking collectives: none -> 24 us  [body(): weight_grad = all_gather(grad_slice, axis_name='rows').sum(axis=0)]
  transfers between devices with their start and end apart: 6 -> 6, of which waited for: 5 -> 5; matrix products, arithmetic and copies ran while one was open for 3% -> 4% of each run, Pallas kernels for 0% -> 0%
where the time goes in v1:
time: 167 us
  waiting for transfers between devices  63.2 us (38%)
  blocking collectives  40.3 us (24%)
  starting transfers between devices  22 us (13%)
  between operations  14.2 us (9%)
  matrix products  11.6 us (7%)
  local copies, waits for them, and re-layouts  9.55 us (6%)
  other arithmetic  5.74 us (3%)
    all_to_all x1, waiting for transfers between devices, body(): lax.all_to_all(partial_value, ('feat', 'rows'), split_axis=0, concat_axis...  33.8 us
    all_gather x1, waiting for transfers between devices, body(): lax.all_gather(pieces, 'feat', axis=0, tiled=True)  24 us
    all_gather x1, blocking collectives, body(): weight_grad = all_gather(grad_slice, axis_name='rows').sum(axis=0)  24 us
    all_to_all x1, blocking collectives, body(): lax.all_to_all(grad_proj.reshape(row_size, sub_rows, hidden_width), 'rows...  16.3 us
    all_to_all x1, starting transfers between devices, body(): lax.all_to_all(partial_value, ('feat', 'rows'), split_axis=0, concat_axis...  11.1 us
    ppermute x2, starting transfers between devices, shifted(): return lax.ppermute(block, axis, route)  5.42 us
    ppermute x1, starting transfers between devices, padded(): lax.ppermute(head, axis, [((i + 1) % count, i) for i in range(count)])  4.74 us
  transfers between devices with their start and end apart: 6, of which 5 were waited for; matrix products, arithmetic and copies ran while one was open for 4% of the time, Pallas kernels for 0%

profile of v1, /device:TPU:0, one launch (start us, length us, event | category | flops | bytes accessed | tf_op | source)
XLA Modules:
  0.0 166.6 jit_solution(13654095066257501739)
XLA Ops:
  7.2 0.0 copy-start
  7.2 0.8 copy-done
  8.0 1.9 %convert_bitcast_fusion.1 = bf16[128,48,256]{0,2,1:T(8,128)(2,1)S(1)} fusion(bf16[16,128,48]{1,2,0:T(8,128)(2,1)} %param.11, bf16[128,256]{1,0:T(8,128)(2,1)S(1)} %copy-done, s32[]{:T(128)S(6)} %select_n.13), kind=kOutput, calls=%fused_computation.4 | convolution fusion | flops 51904512 | bytes 3350532 | tf_op jit(solution)/shard_map/cdn,ch->dnh/dot_general | solution.py:58
  9.9 3.2 %copy.17 = bf16[128,48,256]{2,1,0:T(8,128)(2,1)} copy(bf16[128,48,256]{0,2,1:T(8,128)(2,1)S(1)} %convert_bitcast_fusion.1) | data formatting | bytes 6291456 | tf_op jit(solution)/shard_map/convert_element_type | solution.py:60
  13.1 0.0 copy-start.9
  13.1 0.0 copy-start.8
  13.1 11.1 %all-to-all-start = ((bf16[128,48,256]{2,1,0:T(8,128)(2,1)}), bf16[128,48,256]{2,1,0:T(8,128)(2,1)S(1)}, u32[]{:S(2)}, u32[]{:S(2)}) async-start(bf16[128,48,256]{2,1,0:T(8,128)(2,1)} %copy.17), calls=%async_computation | async-start | bytes 6291456 | tf_op jit(solution)/shard_map/all_to_all | solution.py:61
  24.3 0.0 all-gather.3.cloned.1.call-start
  24.3 0.0 copy-done.9
  24.3 0.1 fusion.27
  24.4 0.0 copy-done.8
  24.4 2.0 %convert_reduce_fusion = (f32[6,128]{1,0:T(8,128)S(1)}, bf16[6,8,128,128]{3,2,1,0:T(8,128)(2,1)S(1)}) fusion(bf16[6,8,128,128]{3,2,1,0:T(8,128)(2,1)} %param.14, bf16[6,8]{1,0:T(8,128)(2,1)S(1)} %fusion.27), kind=kLoop, calls=%fused_computation.3 | loop fusion | flops 2358528 | bytes 3148896 | tf_op jit(solution)/shard_map/reduce_sum | solution.py:74
  26.5 0.0 copy-start.1
  26.5 1.1 copy-done.1
  27.6 3.1 %convert_bitcast_fusion = bf16[10,6,128,128]{3,0,2,1:T(8,128)(2,1)} fusion(bf16[6,8,128,128]{3,2,1,0:T(8,128)(2,1)S(1)} %get-tuple-element.27, s32[6,8]{1,0:T(8,128)S(1)} %get-tuple-element.29), kind=kOutput, calls=%fused_computation.2 | convolution fusion | flops 16712160 | bytes 3539136 | tf_op jit(solution)/shard_map/bkq,bkij->qbij/dot_general | solution.py:90
  30.7 33.8 %all-to-all-done = bf16[128,48,256]{2,1,0:T(8,128)(2,1)S(1)} async-done(((bf16[128,48,256]{2,1,0:T(8,128)(2,1)}), bf16[128,48,256]{2,1,0:T(8,128)(2,1)S(1)}, u32[]{:S(2)}, u32[]{:S(2)}) %all-to-all-start) | async-done | bytes 3145760 | tf_op jit(solution)/shard_map/all_to_all | solution.py:61
  64.5 0.4 bitcast_reduce_fusion
  64.9 0.0 copy-start.4
  65.0 0.7 copy-done.4
  65.7 0.7 collective-permute-start
  66.4 4.7 %collective-permute-start.1 = (bf16[256,256]{1,0:T(8,128)(2,1)S(1)}, bf16[256,256]{1,0:T(8,128)(2,1)S(1)}, u32[]{:S(2)}, u32[]{:S(2)}) collective-permute-start(bf16[256,256]{1,0:T(8,128)(2,1)S(1)} %get-tuple-element.35), channel_id=1, source_target_pairs={{1,0},{2,1},{3,2},{4,3},{5,4},{6,5},{7,6},{8,7},{9,8},{10,9},{11,1... | collective-permute-start | bytes 393224 | tf_op jit(solution)/shard_map/ppermute | solution.py:19
  71.1 0.1 reshape.114
  71.2 2.9 %collective-permute-done = bf16[256,256]{1,0:T(8,128)(2,1)S(1)} collective-permute-done((bf16[256,256]{1,0:T(8,128)(2,1)S(1)}, bf16[256,256]{1,0:T(8,128)(2,1)S(1)}, u32[]{:S(2)}, u32[]{:S(2)}) %collective-permute-start) | collective-permute-done | bytes 131104 | tf_op jit(solution)/shard_map/ppermute | solution.py:17
  74.1 0.0 collective-permute-done.1
  74.1 1.0 pad_maximum_fusion
  75.1 0.0 copy-start.2
  75.1 0.0 copy-start.5
  75.1 0.0 copy-start.10
  75.2 2.5 %gather_fusion = bf16[48,128,256]{2,1,0:T(8,128)(2,1)} fusion(bf16[10,128,256]{2,1,0:T(8,128)(2,1)S(1)} %bitcast.48, s32[1024]{0:T(1024)S(1)} %pad_clamp_fusion), kind=kCustom, calls=%fused_computation | custom fusion | bytes 6291648 | tf_op jit(solution)/shard_map/gather | solution.py:75
  77.7 0.0 copy-done.2
  77.7 0.0 copy-done.5
  77.7 0.0 copy-done.10
  77.7 0.0 copy-start.3
  77.7 0.0 copy-start.7
  77.7 2.8 %fusion.8 = f32[6,128,256]{2,1,0:T(8,128)S(1)} fusion(bf16[6,8,128,128]{3,2,1,0:T(8,128)(2,1)S(1)} %copy-done.2, bf16[6,8,128,256]{3,2,1,0:T(8,128)(2,1)} %bitcast.50, bf16[6,128,256]{2,1,0:T(8,128)(2,1)S(1)} %bitcast.51, f32[256]{0:T(256)S(1)} %copy-done.10, f32[6,128]{1,0:T(8,128)S(1)} %broadcast_add_fusion), kind=kOutput, calls=%fused_computation.12 | convolution fusion | flops 403439616 | bytes 5902336 | tf_op jit(solution)/shard_map/bkij,bkjh->bih/dot_general | solution.py:76
  80.5 0.0 copy-done.3
  80.5 0.1 copy-done.7
  80.6 1.5 fusion.32
  82.1 0.1 collective-permute-start.2
  82.2 0.0 copy-start.6
  82.2 1.4 slice_add_fusion
  83.6 5.3 %collective-permute-start.3 = (bf16[2,128,256]{2,1,0:T(8,128)(2,1)S(1)}, bf16[2,128,256]{2,1,0:T(8,128)(2,1)S(1)}, u32[]{:S(2)}, u32[]{:S(2)}) collective-permute-start(bf16[2,128,256]{2,1,0:T(8,128)(2,1)S(1)} %get-tuple-element.32), channel_id=1, source_target_pairs={{1,0},{2,1},{3,2},{4,3},{5,4},{6,5},{7,6},{8,7},{9,8},{10,9},{11,1... | collective-permute-start | bytes 393224 | tf_op jit(solution)/shard_map/ppermute | solution.py:29
  88.9 1.6 collective-permute-done.2
  90.5 0.1 fusion.19
  90.5 0.9 collective-permute-done.3
  91.4 0.1 fusion.18
  91.5 16.3 %all_to_all.10 = bf16[16,48,256]{2,1,0:T(8,128)(2,1)S(1)} all-to-all(bf16[16,48,256]{2,1,0:T(8,128)(2,1)S(1)} %bitcast.52), channel_id=1, replica_groups=mesh['feat'=8,'rows'=16] {'rows'}, dimensions={0} | all-to-all | bytes 786432 | tf_op jit(solution)/shard_map/all_to_all | solution.py:102
  107.9 0.9 copy.20
  108.8 0.0 all-gather.3.cloned.1.call-update
  108.8 24.0 %all-gather.3.cloned.1.call-done = bf16[128,48,256]{2,0,1:T(8,128)(2,1)} async-done(((bf16[16,48,256]{2,0,1:T(8,128)(2,1)}), bf16[128,48,256]{2,0,1:T(8,128)(2,1)}) %all-gather.3.cloned.1.call-update) | async-done | bytes 3145744 | tf_op jit(solution)/shard_map/all_gather | solution.py:112
  132.8 0.0 copy-done.6
  132.8 2.4 %convolution_bitcast_fusion.1 = f32[16,256]{1,0:T(8,128)S(1)} fusion(bf16[128,48,256]{2,0,1:T(8,128)(2,1)} %all-gather.3.cloned.1.call-done, bf16[16,128,48]{1,2,0:T(8,128)(2,1)S(1)} %copy-done.6), kind=kOutput, calls=%fused_computation.15 | convolution fusion | flops 50331648 | bytes 3358720 | tf_op jit(solution)/shard_map/cdn,dnh->ch/dot_general | solution.py:109
  135.2 24.0 %all-gather = f32[256,256]{1,0:T(8,128)S(1)} all-gather(f32[16,256]{1,0:T(8,128)S(1)} %convolution_bitcast_fusion.1), channel_id=2, replica_groups=mesh['feat'=8,'rows'=16] {'rows'}, dimensions={0}, use_global_device_ids=true | all-gather | bytes 278528 | tf_op jit(solution)/shard_map/all_gather | solution.py:115
  159.2 0.6 reduce_sum.32
  (6 shorter events, 0.1 us)
Async XLA Ops:
  7.2 0.8 copy-start
  13.1 11.2 %copy-start.9 = (s32[6]{0:T(128)S(1)}, s32[6]{0:T(128)}, u32[]{:S(2)}) copy-start(s32[6]{0:T(128)} %param.16) | copy-start | bytes 76
  13.1 11.3 %copy-start.8 = (s32[6,8]{1,0:T(8,128)S(1)}, s32[6,8]{1,0:T(8,128)}, u32[]{:S(2)}) copy-start(s32[6,8]{1,0:T(8,128)} %param.15) | copy-start | bytes 580
  13.1 51.4 %all-to-all-start = ((bf16[128,48,256]{2,1,0:T(8,128)(2,1)}), bf16[128,48,256]{2,1,0:T(8,128)(2,1)S(1)}, u32[]{:S(2)}, u32[]{:S(2)}) async-start(bf16[128,48,256]{2,1,0:T(8,128)(2,1)} %copy.17), calls=%async_computation | async-start | bytes 6291456 | tf_op jit(solution)/shard_map/all_to_all | solution.py:61
  24.3 108.5 %all-gather.3.cloned.1.call-start = ((), (), s32[]{:S(2)}) async-start(), calls=%async_computation.2 | async-start | bytes 3538944 | tf_op jit(solution)/shard_map/all_gather | solution.py:112
  26.5 1.1 copy-start.1
  64.9 0.7 copy-start.4
  65.7 8.4 %collective-permute-start = (bf16[256,256]{1,0:T(8,128)(2,1)S(1)}, bf16[256,256]{1,0:T(8,128)(2,1)S(1)}, u32[]{:S(2)}, u32[]{:S(2)}) collective-permute-start(bf16[256,256]{1,0:T(8,128)(2,1)S(1)} %get-tuple-element.34), channel_id=1, source_target_pairs={{0,1},{1,2},{2,3},{3,4},{4,5},{5,6},{6,7},{7,8},{8,9},{9,10},{10,1... | collective-permute-start | bytes 393224 | tf_op jit(solution)/shard_map/ppermute | solution.py:17
  66.4 7.7 %collective-permute-start.1 = (bf16[256,256]{1,0:T(8,128)(2,1)S(1)}, bf16[256,256]{1,0:T(8,128)(2,1)S(1)}, u32[]{:S(2)}, u32[]{:S(2)}) collective-permute-start(bf16[256,256]{1,0:T(8,128)(2,1)S(1)} %get-tuple-element.35), channel_id=1, source_target_pairs={{1,0},{2,1},{3,2},{4,3},{5,4},{6,5},{7,6},{8,7},{9,8},{10,9},{11,1... | collective-permute-start | bytes 393224 | tf_op jit(solution)/shard_map/ppermute | solution.py:19
  75.1 2.6 %copy-start.2 = (bf16[6,8,128,128]{3,2,1,0:T(8,128)(2,1)S(1)}, bf16[6,8,128,128]{3,2,1,0:T(8,128)(2,1)}, u32[]{:S(2)}) copy-start(bf16[6,8,128,128]{3,2,1,0:T(8,128)(2,1)} %copy-done.1) | copy-start | bytes 4718596
  75.1 2.6 %copy-start.5 = (bf16[768,256]{1,0:T(8,128)(2,1)S(1)}, bf16[768,256]{1,0:T(8,128)(2,1)}, u32[]{:S(2)}) copy-start(bf16[768,256]{1,0:T(8,128)(2,1)} %copy-done.4) | copy-start | bytes 1179652
  75.1 2.6 %copy-start.10 = (f32[256]{0:T(256)S(1)}, f32[256]{0:T(256)}, u32[]{:S(2)}) copy-start(f32[256]{0:T(256)} %param.13) | copy-start | bytes 3076
  77.7 2.8 %copy-start.3 = (bf16[10,6,128,128]{3,0,2,1:T(8,128)(2,1)S(1)}, bf16[10,6,128,128]{3,0,2,1:T(8,128)(2,1)}, u32[]{:S(2)}) copy-start(bf16[10,6,128,128]{3,0,2,1:T(8,128)(2,1)} %convert_bitcast_fusion) | copy-start | bytes 5898244
  77.7 2.9 %copy-start.7 = (bf16[768,256]{1,0:T(8,128)(2,1)S(1)}, bf16[768,256]{1,0:T(8,128)(2,1)}, u32[]{:S(2)}) copy-start(bf16[768,256]{1,0:T(8,128)(2,1)} %param.17) | copy-start | bytes 1179652
  82.1 8.4 %collective-permute-start.2 = (bf16[2,128,256]{2,1,0:T(8,128)(2,1)S(1)}, bf16[2,128,256]{2,1,0:T(8,128)(2,1)S(1)}, u32[]{:S(2)}, u32[]{:S(2)}) collective-permute-start(bf16[2,128,256]{2,1,0:T(8,128)(2,1)S(1)} %get-tuple-element.33), channel_id=1, source_target_pairs={{15,0},{0,1},{1,2},{2,3},{3,4},{4,5},{5,6},{6,7},{7,8},{8,9},{9,10... | collective-permute-start | bytes 393224 | tf_op jit(solution)/shard_map/ppermute | solution.py:29
  82.2 50.6 %copy-start.6 = (bf16[16,128,48]{1,2,0:T(8,128)(2,1)S(1)}, bf16[16,128,48]{1,2,0:T(8,128)(2,1)}, u32[]{:S(2)}) copy-start(bf16[16,128,48]{1,2,0:T(8,128)(2,1)} %param.11) | copy-start | bytes 589828
  83.6 7.9 %collective-permute-start.3 = (bf16[2,128,256]{2,1,0:T(8,128)(2,1)S(1)}, bf16[2,128,256]{2,1,0:T(8,128)(2,1)S(1)}, u32[]{:S(2)}, u32[]{:S(2)}) collective-permute-start(bf16[2,128,256]{2,1,0:T(8,128)(2,1)S(1)} %get-tuple-element.32), channel_id=1, source_target_pairs={{1,0},{2,1},{3,2},{4,3},{5,4},{6,5},{7,6},{8,7},{9,8},{10,9},{11,1... | collective-permute-start | bytes 393224 | tf_op jit(solution)/shard_map/ppermute | solution.py:29
Sparse Core Ops, SparseCore 0:
  108.9 23.8 all-gather.2
